TPU v7x, 128 devices: a whole 4x4x4 slice. The times are simulated.
128 devices in a mesh: expert: 4 (over y), feat: 32 (over x, z, core).
Axes of the slice: x: 4, y: 4, z: 4, core: 2. Of those that a mesh axis runs over, the one named last changes fastest.
Arguments:
- tokens: bfloat16 [1024, 4096], P(('expert', 'feat')), may hold values from -6 to 6
- expert_ids: int32 [1024, 2], P(('expert', 'feat')), may hold values from 0 to 7, as said below
- route_weights: bfloat16 [1024, 2], P(('expert', 'feat')), may hold values from 0.099609375 to 1
- gate_proj: bfloat16 [4096, 28672], P(None, ('expert', 'feat')), may hold values from -0.09375 to 0.09375
- up_proj: bfloat16 [4096, 28672], P(None, ('expert', 'feat')), may hold values from -0.09375 to 0.09375
- down_proj: bfloat16 [28672, 4096], P(('expert', 'feat')), may hold values from -0.046875 to 0.046875
- enc_weight: float32 [4096, 32768], P(None, ('expert', 'feat')), may hold values from -0.09375 to 0.09375
- enc_bias: float32 [32768], P(('expert', 'feat')), may hold values from -3 to 3
- log_threshold: float32 [32768], P(('expert', 'feat')), may hold values from -2.3 to 0
- dec_weight: float32 [32768, 4096], P(('expert', 'feat')), may hold values from -0.046875 to 0.046875
Outputs:
- grad_encoder: float32 [4096, 32768], P(None, ('expert', 'feat'))
- grad_decoder: float32 [32768, 4096], P(('expert', 'feat'))
- grad_bias: float32 [32768], P(('expert', 'feat'))
- grad_threshold: float32 [32768], P(('expert', 'feat'))
Inputs may be any that keep to these rules, and one draw needn't show every extreme that they name: `expert_ids`: each token names two different experts of 0 to 7. Among the 8 tokens of one device, each expert below 2 is named by at most 4 tokens; in every draw one of these experts, drawn from the seed and the same for all devices, is named by exactly 4 tokens of every device.
All inputs are finite; a program needn't handle non-finite values.
Results may differ from a plain program's by a relative error of at most 0.0021.
Values may be sent and summed in bfloat16 or wider, within the bound.
A program may use at most 128 MiB of HBM per device.

v0:
```python
import jax
import jax.numpy as jnp
from jax import lax
from jax.sharding import PartitionSpec as P

sharpness = 0.1
kernel_width = 0.5
density_weight = 0.01


def partner(block, axis, stride):
    count = lax.axis_size(axis)
    route = []
    for low in range(count):
        high = low | 1 << stride
        if high != low and high < count:
            route += [(low, high), (high, low)]
    return lax.ppermute(block, axis, route)


def pack_slots(tokens, expert_ids, route_weights, experts):
    capacity = tokens.shape[0] // 2
    window = jnp.arange(experts, dtype=jnp.int32)
    matches = expert_ids[:, :, None] == window[None, None, :]
    named = jnp.sum(matches.astype(jnp.int32), axis=1)
    weighted = jnp.sum(
        jnp.where(matches, route_weights[:, :, None], jnp.zeros((), jnp.bfloat16)), axis=1
    )
    rows = jnp.arange(tokens.shape[0], dtype=jnp.int32)
    earlier = rows[None, :, None] < rows[:, None, None]
    slot_index = jnp.sum(jnp.where(earlier, named[None, :, :], 0), axis=1)
    places = jnp.arange(capacity, dtype=jnp.int32)
    chosen = (named.T[:, None, :] == 1) & (slot_index.T[:, None, :] == places[None, :, None])
    slot_rows = jnp.einsum(
        "ect,td->ecd", chosen.astype(jnp.bfloat16), tokens, preferred_element_type=jnp.float32
    ).astype(jnp.bfloat16)
    slot_weights = jnp.sum(
        jnp.where(chosen, weighted.T[:, None, :], jnp.zeros((), jnp.bfloat16)), axis=2
    )
    return (slot_rows, slot_weights)


def split(value):
    high = lax.reduce_precision(value, 8, 7)
    return (high.astype(jnp.bfloat16), (value - high).astype(jnp.bfloat16))


def product(left, right, dims):
    return lax.dot_general(left, right, (dims, ((), ())), preferred_element_type=jnp.float32)


def body(
    tokens,
    expert_ids,
    route_weights,
    gate_proj,
    up_proj,
    down_proj,
    enc_weight,
    enc_bias,
    log_threshold,
    dec_weight,
):
    copies = 2
    experts = lax.axis_size("expert") // copies
    slot_rows, slot_weights = pack_slots(tokens, expert_ids, route_weights, experts)
    send_rows = jnp.repeat(slot_rows, copies, axis=0)
    send_weights = jnp.repeat(slot_weights, copies, axis=0)
    came_rows, came_weights = (
        lax.all_to_all(send_rows, "expert", split_axis=0, concat_axis=0, tiled=True),
        lax.all_to_all(send_weights, "expert", split_axis=0, concat_axis=0, tiled=True),
    )
    all_rows, all_weights = (
        lax.all_gather(came_rows, "feat", axis=0, tiled=True),
        lax.all_gather(came_weights, "feat", axis=0, tiled=True),
    )
    width = tokens.shape[1]
    token_rows = all_rows.reshape(-1, width)
    row_weights = all_weights.reshape(-1).astype(jnp.float32)
    gate_act = jnp.dot(token_rows, gate_proj, preferred_element_type=jnp.float32)
    up_act = jnp.dot(token_rows, up_proj, preferred_element_type=jnp.float32)
    hidden = (jax.nn.silu(gate_act) * up_act).astype(jnp.bfloat16)
    target_part = jnp.dot(hidden, down_proj, preferred_element_type=jnp.float32)
    rows = ((1,), (0,))
    down = ((0,), (0,))
    enc_high, enc_low = split(enc_weight)
    dec_high, dec_low = split(dec_weight)
    preact = product(token_rows, enc_high, rows) + product(token_rows, enc_low, rows) + enc_bias
    threshold = jnp.exp(log_threshold)
    shifted = preact - threshold
    soft_gate = jax.nn.sigmoid(shifted / sharpness)
    active = preact * soft_gate
    act_high, act_low = split(active)
    recon = product(act_high, dec_high, rows) + product(act_high, dec_low, rows)
    partial_error = recon + product(act_low, dec_high, rows) - target_part
    feat_total = lax.psum_scatter(partial_error, "feat", scatter_dimension=0, tiled=True)
    recon_error = feat_total + partner(feat_total, "expert", 0)
    own_rows = feat_total.shape[0]
    own_weights = lax.dynamic_slice_in_dim(row_weights, lax.axis_index("feat") * own_rows, own_rows)
    own_grad = (2.0 * own_weights[:, None] * recon_error).astype(jnp.bfloat16)
    residual_grad = lax.all_gather(own_grad, "feat", axis=0, tiled=True)
    grad_decoder = product(act_high, residual_grad, down) + product(act_low, residual_grad, down)
    across = ((1,), (1,))
    grad_active = product(residual_grad, dec_high, across) + product(residual_grad, dec_low, across)
    grad_pre = grad_active * soft_gate
    pre_high, pre_low = split(grad_pre)
    grad_encoder = product(token_rows, pre_high, down) + product(token_rows, pre_low, down)
    grad_bias = jnp.sum(grad_pre, axis=0)
    kernel = jnp.maximum(0.0, 1.0 - jnp.abs(shifted) / kernel_width) / kernel_width
    slope_sum = jnp.sum(
        (grad_active * threshold + density_weight * row_weights[:, None]) * kernel, axis=0
    )
    grad_threshold = -threshold * slope_sum
    return (grad_encoder, grad_decoder, grad_bias, grad_threshold)


def solution(mesh):
    in_specs = (
        P(("expert", "feat"), None),
        P(("expert", "feat"), None),
        P(("expert", "feat"), None),
        P(None, ("expert", "feat")),
        P(None, ("expert", "feat")),
        P(("expert", "feat"), None),
        P(None, ("expert", "feat")),
        P(("expert", "feat")),
        P(("expert", "feat")),
        P(("expert", "feat"), None),
    )
    out_specs = (
        P(None, ("expert", "feat")),
        P(("expert", "feat"), None),
        P(("expert", "feat")),
        P(("expert", "feat")),
    )
    return jax.shard_map(body, mesh=mesh, in_specs=in_specs, out_specs=out_specs, check_vma=False)
```

profile of v0, /device:TPU:1, one launch (start us, length us, event | category | flops | bytes accessed | tf_op | source)
XLA Modules:
  0.0 313.5 jit_solution(17543353753348144969)
XLA Ops:
  7.2 0.0 copy-start
  7.2 0.0 all-gather.4.cloned.1.call-start
  7.2 0.8 convert_reduce_fusion.1
  8.1 0.1 select_reduce_fusion
  8.2 1.0 convolution_convert_fusion
  9.3 9.7 %all_to_all.17 = bf16[4,4,4096]{2,1,0:T(4,128)(2,1)} all-to-all(bf16[4,4,4096]{2,1,0:T(4,128)(2,1)S(1)} %bitcast.22), channel_id=1, replica_groups=mesh['expert'=4,'feat'=32] {'expert'}, dimensions={0} | all-to-all | bytes 262144 | tf_op jit(solution)/shard_map/all_to_all | solution.py:70
  19.0 0.0 all-gather.4.cloned.1.call-update
  19.0 0.0 reduce-scatter.2.cloned.1.call-start
  19.1 0.7 exp.10
  19.8 48.0 %all-gather.4.cloned.1.call-done = bf16[128,4,4096]{2,1,0:T(4,128)(2,1)} async-done(((bf16[4,4,4096]{2,1,0:T(4,128)(2,1)}), bf16[128,4,4096]{2,1,0:T(4,128)(2,1)}) %all-gather.4.cloned.1.call-update) | async-done | bytes 4194320 | tf_op jit(solution)/shard_map/all_gather | solution.py:74
  67.8 6.9 %reshape.55 = bf16[512,4096]{1,0:T(8,128)(2,1)} reshape(bf16[128,4,4096]{2,1,0:T(4,128)(2,1)} %all-gather.4.cloned.1.call-done) | data formatting | bytes 8388608 | tf_op jit(solution)/shard_map/reshape | solution.py:78
  74.6 0.0 copy-start.7
  74.6 0.0 copy-start.8
  74.6 4.9 %fusion.2 = f32[512,256]{1,0:T(8,128)S(1)} fusion(bf16[512,4096]{1,0:T(8,128)(2,1)} %reshape.55, f32[4096,256]{1,0:T(8,128)} %param.16), kind=kOutput, calls=%fused_computation.10 | convolution fusion | flops 1076887552 | bytes 8912896 | tf_op jit(solution)/shard_map/dot_general | solution.py:49
  79.5 0.0 copy-done.2
  79.5 1.0 copy-done.7
  80.6 0.0 copy-done.8
  80.6 0.0 copy-start.5
  80.6 1.3 fusion.6
  81.8 0.9 copy-done.5
  82.8 4.6 %fusion.11 = f32[512,4096]{1,0:T(8,128)} fusion(f32[256,4096]{1,0:T(8,128)S(1)} %copy-done.5, f32[512,256]{1,0:T(8,128)S(1)} %fusion.6, f32[256]{0:T(256)S(1)} %exp.10), kind=kOutput, calls=%fused_computation.23 | convolution fusion | flops 1077936128 | bytes 13108224 | tf_op jit(solution)/shard_map/dot_general | solution.py:49
  87.3 0.0 copy-start.12
  87.3 4.5 %fusion.38 = f32[512,4096]{1,0:T(8,128)} fusion(f32[256,4096]{1,0:T(8,128)S(1)} %copy-done.5, f32[512,256]{1,0:T(8,128)S(1)} %fusion.6, f32[256]{0:T(256)S(1)} %exp.10), kind=kOutput, calls=%fused_computation.58 | convolution fusion | flops 1076887552 | bytes 13108224 | tf_op jit(solution)/shard_map/dot_general | solution.py:49
  91.9 0.0 copy-done.12
  91.9 1.4 fusion.46
  93.3 0.0 copy-done
  93.3 8.7 %fusion.8 = f32[512,4096]{1,0:T(8,128)} fusion(bf16[224,4096]{1,0:T(8,128)(2,1)S(1)} %copy-done, bf16[512,4096]{1,0:T(8,128)(2,1)} %reshape.55, bf16[4096,224]{0,1:T(8,128)(2,1)} %param.14, f32[512,224]{0,1:T(8,128)S(1)} %fusion.46), kind=kOutput, calls=%fused_computation.17 | convolution fusion | flops 1879736320 | bytes 16711680 | tf_op jit(solution)/shard_map/dot_general | solution.py:83
  102.0 14.3 %add_subtract_fusion = f32[512,4096]{1,0:T(8,128)} fusion(f32[512,4096]{1,0:T(8,128)} %fusion.8, f32[512,4096]{1,0:T(8,128)} %fusion.38, f32[512,4096]{1,0:T(8,128)} %fusion.11, f32[256,4096]{1,0:T(8,128)} %param.19, f32[512,256]{1,0:T(8,128)S(1)} %fusion.6, f32[256]{0:T(256)S(1)} %exp.10), kind=kOutput, calls=%fused_computation | convolution fusion | flops 1083310080 | bytes 38274048 | tf_op jit(solution)/shard_map/dot_general | solution.py:49
  116.3 0.0 copy-start.10
  116.3 0.0 copy-start.11
  116.3 0.0 reduce-scatter.2.cloned.1.call-update
  116.3 0.7 copy-done.10
  117.0 0.0 copy-done.11
  117.0 89.5 %reduce-scatter.2.cloned.1.call-done = f32[16,4096]{1,0:T(8,128)} async-done(((f32[512,4096]{1,0:T(8,128)}), f32[16,4096]{1,0:T(8,128)}) %reduce-scatter.2.cloned.1.call-update) | async-done | bytes 262160 | tf_op jit(solution)/shard_map/reduce_scatter | solution.py:96
  206.5 1.2 collective-permute-start
  207.7 0.1 fusion.32
  207.8 0.6 copy.24
  208.4 3.7 %all-to-all-start.1 = ((bf16[4,1,4]{2,1,0:T(2,128)(2,1)}), bf16[4,1,4]{2,1,0:T(2,128)(2,1)S(1)}, u32[]{:S(2)}, u32[]{:S(2)}) async-start(bf16[4,1,4]{2,1,0:T(2,128)(2,1)} %copy.24), calls=%async_computation.1 | async-start | bytes 4096 | tf_op jit(solution)/shard_map/all_to_all | solution.py:71
  212.1 0.0 all-gather.6.cloned.1.call-start
  212.1 4.1 %all-to-all-done.1 = bf16[4,1,4]{2,1,0:T(2,128)(2,1)S(1)} async-done(((bf16[4,1,4]{2,1,0:T(2,128)(2,1)}), bf16[4,1,4]{2,1,0:T(2,128)(2,1)S(1)}, u32[]{:S(2)}, u32[]{:S(2)}) %all-to-all-start.1) | async-done | bytes 64 | tf_op jit(solution)/shard_map/all_to_all | solution.py:71
  216.2 27.5 %all-gather = bf16[128,1,4]{2,1,0:T(2,128)(2,1)S(1)} all-gather(bf16[4,1,4]{2,1,0:T(2,128)(2,1)S(1)} %all-to-all-done.1), channel_id=2, replica_groups=mesh['expert'=4,'feat'=32] {'feat'}, dimensions={0}, use_global_device_ids=true | all-gather | bytes 1056 | tf_op jit(solution)/shard_map/all_gather | solution.py:75
  243.7 0.2 convert_reduce_fusion
  243.9 0.1 reshape.56
  244.0 0.1 dynamic-slice_multiply_fusion
  244.1 0.0 collective-permute-done
  244.1 1.7 multiply_convert_fusion
  245.8 0.0 all-gather.6.cloned.1.call-update
  245.8 43.2 %all-gather.6.cloned.1.call-done = bf16[512,4096]{1,0:T(8,128)(2,1)} async-done(((bf16[16,4096]{1,0:T(8,128)(2,1)}), bf16[512,4096]{1,0:T(8,128)(2,1)}) %all-gather.6.cloned.1.call-update) | async-done | bytes 4194320 | tf_op jit(solution)/shard_map/all_gather | solution.py:101
  289.0 0.0 copy-start.4
  289.0 0.0 copy-start.6
  289.0 4.9 %fusion.9 = f32[512,256]{1,0:T(8,128)S(1)} fusion(bf16[512,4096]{1,0:T(8,128)(2,1)} %all-gather.6.cloned.1.call-done, f32[256,4096]{1,0:T(8,128)} %param.19), kind=kOutput, calls=%fused_computation.22 | convolution fusion | flops 1076887552 | bytes 8912896 | tf_op jit(solution)/shard_map/dot_general | solution.py:49
  293.9 0.0 copy-done.4
  293.9 1.0 copy-done.6
  294.9 0.0 copy-start.9
  294.9 0.0 copy-start.3
  294.9 2.0 fusion.44
  296.9 0.0 copy-done.9
  296.9 0.6 negate_multiply_fusion
  297.5 0.0 copy-done.3
  297.5 1.3 fusion.23
  298.8 3.3 %convolution_add_fusion.1 = f32[4096,256]{1,0:T(8,128)} fusion(f32[4096,256]{1,0:T(8,128)S(1)} %fusion.23, bf16[512,4096]{1,0:T(8,128)(2,1)S(1)} %copy-done.3, f32[512,256]{1,0:T(8,128)S(1)} %get-tuple-element.5), kind=kOutput, calls=%fused_computation.6 | convolution fusion | flops 1075183616 | bytes 13107200 | tf_op jit(solution)/shard_map/dot_general | solution.py:49
  302.1 1.4 fusion.25
  303.5 3.5 %convolution_add_fusion = f32[256,4096]{1,0:T(8,128)} fusion(f32[256,4096]{1,0:T(8,128)S(1)} %fusion.25, bf16[512,4096]{1,0:T(8,128)(2,1)S(1)} %copy-done.4, f32[512,256]{1,0:T(8,128)S(1)} %fusion.6, f32[256]{0:T(256)S(1)} %exp.10), kind=kOutput, calls=%fused_computation.5 | convolution fusion | flops 1075838976 | bytes 13108224 | tf_op jit(solution)/shard_map/dot_general | solution.py:49
  307.0 0.0 copy-done.1
  (8 shorter events, 0.1 us)
Async XLA Ops:
  7.2 86.1 %copy-start = (bf16[224,4096]{1,0:T(8,128)(2,1)S(1)}, bf16[224,4096]{1,0:T(8,128)(2,1)}, u32[]{:S(2)}) copy-start(bf16[224,4096]{1,0:T(8,128)(2,1)} %param.15) | copy-start | bytes 5505028
  7.2 60.6 %all-gather.4.cloned.1.call-start = ((), (), s32[]{:S(2)}) async-start(), calls=%async_computation.3 | async-start | bytes 4325376 | tf_op jit(solution)/shard_map/all_gather | solution.py:74
  19.0 187.5 %reduce-scatter.2.cloned.1.call-start = ((), (), s32[]{:S(2)}) async-start(), calls=%async_computation.4 | async-start | bytes 8650752 | tf_op jit(solution)/shard_map/reduce_scatter | solution.py:96
  74.6 4.9 %copy-start.2 = (bf16[512,4096]{1,0:T(8,128)(2,1)S(1)}, bf16[512,4096]{1,0:T(8,128)(2,1)}, u32[]{:S(2)}) copy-start(bf16[512,4096]{1,0:T(8,128)(2,1)} %reshape.55) | copy-start | bytes 12582916
  74.6 5.9 %copy-start.7 = (f32[4096,256]{1,0:T(8,128)S(1)}, f32[4096,256]{1,0:T(8,128)}, u32[]{:S(2)}) copy-start(f32[4096,256]{1,0:T(8,128)} %param.16) | copy-start | bytes 12582916
  74.6 5.9 %copy-start.8 = (f32[256]{0:T(256)S(1)}, f32[256]{0:T(256)}, u32[]{:S(2)}) copy-start(f32[256]{0:T(256)} %param.17) | copy-start | bytes 3076
  80.6 2.2 copy-start.5
  87.3 4.5 %copy-start.12 = (bf16[4096,224]{0,1:T(8,128)(2,1)S(1)}, bf16[4096,224]{0,1:T(8,128)(2,1)}, u32[]{:S(2)}) copy-start(bf16[4096,224]{0,1:T(8,128)(2,1)} %param.13) | copy-start | bytes 5505028
  116.3 0.7 copy-start.10
  116.3 0.7 copy-start.11
  206.5 37.6 %collective-permute-start = (f32[16,4096]{1,0:T(8,128)}, f32[16,4096]{1,0:T(8,128)S(1)}, u32[]{:S(2)}, u32[]{:S(2)}) collective-permute-start(f32[16,4096]{1,0:T(8,128)} %reduce-scatter.2.cloned.1.call-done), channel_id=1, source_target_pairs={{0,32},{32,0},{64,96},{96,64},{1,33},{33,1},{65,97},{97,65},{2,34}... | collective-permute-start | bytes 786440 | tf_op jit(solution)/shard_map/ppermute | solution.py:18
  208.4 7.8 %all-to-all-start.1 = ((bf16[4,1,4]{2,1,0:T(2,128)(2,1)}), bf16[4,1,4]{2,1,0:T(2,128)(2,1)S(1)}, u32[]{:S(2)}, u32[]{:S(2)}) async-start(bf16[4,1,4]{2,1,0:T(2,128)(2,1)} %copy.24), calls=%async_computation.1 | async-start | bytes 4096 | tf_op jit(solution)/shard_map/all_to_all | solution.py:71
  212.1 76.9 %all-gather.6.cloned.1.call-start = ((), (), s32[]{:S(2)}) async-start(), calls=%async_computation.5 | async-start | bytes 4325376 | tf_op jit(solution)/shard_map/all_gather | solution.py:101
  289.0 4.9 %copy-start.4 = (bf16[512,4096]{1,0:T(8,128)(2,1)S(1)}, bf16[512,4096]{1,0:T(8,128)(2,1)}, u32[]{:S(2)}) copy-start(bf16[512,4096]{1,0:T(8,128)(2,1)} %all-gather.6.cloned.1.call-done) | copy-start | bytes 12582916
  289.0 5.9 %copy-start.6 = (f32[256,4096]{1,0:T(8,128)S(1)}, f32[256,4096]{1,0:T(8,128)}, u32[]{:S(2)}) copy-start(f32[256,4096]{1,0:T(8,128)} %param.19) | copy-start | bytes 12582916
  294.9 2.0 copy-start.9
  294.9 2.6 copy-start.3
  302.1 4.9 %copy-start.1 = (bf16[224,4096]{1,0:T(8,128)(2,1)S(1)}, bf16[224,4096]{1,0:T(8,128)(2,1)}, u32[]{:S(2)}) copy-start(bf16[224,4096]{1,0:T(8,128)(2,1)} %param.15) | copy-start | bytes 5505028
Sparse Core Ops, SparseCore 0:
  19.1 48.5 all-gather.3
  116.5 89.9 reduce-scatter.1
  245.9 43.0 all-gather.5
where the time goes:
time: 314 us
  waiting for transfers between devices  185 us (59%)
  matrix products  57.1 us (18%)
  blocking collectives  37.3 us (12%)
  between operations  13.9 us (4%)
  local copies, waits for them, and re-layouts  11.9 us (4%)
  starting transfers between devices  4.98 us (2%)
  other arithmetic  3.61 us (1%)
    reduce_scatter x1, waiting for transfers between devices, body(): lax.psum_scatter(partial_error, 'feat', scatter_dimension=0, tiled=True)  89.5 us
    all_gather x1, waiting for transfers between devices, body(): lax.all_gather(came_rows, 'feat', axis=0, tiled=True)  48 us
    dot_general x11, matrix products, product(): lax.dot_general(left, right, (dims, ((), ())), preferred_element_type=jnp...  45.9 us
    all_gather x1, waiting for transfers between devices, body(): residual_grad = lax.all_gather(own_grad, 'feat', axis=0, tiled=True)  43.2 us
    all_gather x1, blocking collectives, body(): lax.all_gather(came_weights, 'feat', axis=0, tiled=True)  27.5 us
    all_to_all x1, blocking collectives, body(): lax.all_to_all(send_rows, 'expert', split_axis=0, concat_axis=0, tiled=True)  9.75 us
    dot_general x1, matrix products, body(): target_part = jnp.dot(hidden, down_proj, preferred_element_type=jnp.float32)  8.72 us
    reshape x1, local copies, waits for them, and re-layouts, body(): token_rows = all_rows.reshape(-1, width)  6.87 us
  transfers between devices with their start and end apart: 5, of which 4 were waited for; matrix products, arithmetic and copies ran while one was open for 1% of the time, Pallas kernels for 0%

commit v1 on v0

--- a/solution.py
+++ b/solution.py
@@ -6,6 +6,28 @@
 sharpness = 0.1
 kernel_width = 0.5
 density_weight = 0.01
+
+
+def laid_out(parts, dim):
+    lengths = list(parts.shape[1:])
+    lengths[dim] *= parts.shape[0]
+    return jnp.moveaxis(parts, 0, dim).reshape(lengths)
+
+
+def grow_blocks(value, axis):
+    size = lax.axis_size(axis)
+    pieces = value[None]
+    for level in range(size.bit_length() - 1):
+        apart = 1 << level
+        other = lax.ppermute(pieces, axis, [(i, i ^ apart) for i in range(size)])
+        both = jnp.stack([pieces, other])
+        upper = lax.axis_index(axis) >> level & 1
+        pieces = jnp.where(upper == 0, both, both[::-1]).reshape(-1, *value.shape)
+    return pieces
+
+
+def collect(x, axis, dim):
+    return laid_out(grow_blocks(x, axis), dim)
 
 
 def partner(block, axis, stride):
@@ -72,7 +94,7 @@
     )
     all_rows, all_weights = (
         lax.all_gather(came_rows, "feat", axis=0, tiled=True),
-        lax.all_gather(came_weights, "feat", axis=0, tiled=True),
+        collect(came_weights, "feat", 0),
     )
     width = tokens.shape[1]
     token_rows = all_rows.reshape(-1, width)

time: 314 us -> 288 us (0.917)
  blocking collectives: 37.3 us -> 9.75 us
  starting transfers between devices: 4.98 us -> 12.4 us
  waiting for transfers between devices: 185 us -> 178 us
    all_gather x1 -> x0, blocking collectives: 27.5 us -> none  [body(): lax.all_gather(came_weights, 'feat', axis=0, tiled=True)]
    reduce_scatter x1, waiting for transfers between devices: 89.5 us -> 64.7 us  [body(): lax.psum_scatter(partial_error, 'feat', scatter_dimension=0, tiled=True)]
    ppermute x0 -> x5, waiting for transfers between devices: none -> 8.4 us  [grow_blocks(): other = lax.ppermute(pieces, axis, [(i, i ^ apart) for i in range(size)])]
    ppermute x0 -> x5, starting transfers between devices: none -> 7.1 us  [grow_blocks(): other = lax.ppermute(pieces, axis, [(i, i ^ apart) for i in range(size)])]
    all_gather x1, waiting for transfers between devices: 43.2 us -> 49.1 us  [body(): residual_grad = lax.all_gather(own_grad, 'feat', axis=0, tiled=True)]
    ppermute x1, waiting for transfers between devices: 0.01 us -> 3.89 us  [partner(): return lax.ppermute(block, axis, route)]
  transfers between devices with their start and end apart: 5 -> 10, of which waited for: 4 -> 10; matrix products, arithmetic and copies ran while one was open for 1% -> 1% of each run, Pallas kernels for 0% -> 0%
where the time goes in v1:
time: 288 us; the launch traced here: 287 us
  waiting for transfers between devices  178 us (62%)
  matrix products  57.1 us (20%)
  between operations  13.9 us (5%)
  local copies, waits for them, and re-layouts  12.5 us (4%)
  starting transfers between devices  12.4 us (4%)
  blocking collectives  9.75 us (3%)
  other arithmetic  3.51 us (1%)
    reduce_scatter x1, waiting for transfers between devices, body(): lax.psum_scatter(partial_error, 'feat', scatter_dimension=0, tiled=True)  64.7 us
    all_gather x1, waiting for transfers between devices, body(): residual_grad = lax.all_gather(own_grad, 'feat', axis=0, tiled=True)  49.1 us
    all_gather x1, waiting for transfers between devices, body(): lax.all_gather(came_rows, 'feat', axis=0, tiled=True)  48 us
    dot_general x11, matrix products, product(): lax.dot_general(left, right, (dims, ((), ())), preferred_element_type=jnp...  45.9 us
    all_to_all x1, blocking collectives, body(): lax.all_to_all(send_rows, 'expert', split_axis=0, concat_axis=0, tiled=True)  9.75 us
    dot_general x1, matrix products, body(): target_part = jnp.dot(hidden, down_proj, preferred_element_type=jnp.float32)  8.71 us
    ppermute x5, waiting for transfers between devices, grow_blocks(): other = lax.ppermute(pieces, axis, [(i, i ^ apart) for i in range(size)])  8.4 us
    ppermute x5, starting transfers between devices, grow_blocks(): other = lax.ppermute(pieces, axis, [(i, i ^ apart) for i in range(size)])  7.1 us
  transfers between devices with their start and end apart: 10, of which 10 were waited for; matrix products, arithmetic and copies ran while one was open for 1% of the time, Pallas kernels for 0%

profile of v1, /device:TPU:1, one launch (start us, length us, event | category | flops | bytes accessed | tf_op | source)
XLA Modules:
  0.0 287.3 jit_solution(11591524021181020678)
XLA Ops:
  7.2 0.0 copy-start
  7.2 0.0 all-gather.3.cloned.1.call-start
  7.2 0.8 convert_reduce_fusion
  8.1 0.1 select_reduce_fusion
  8.2 1.0 convolution_convert_fusion
  9.3 9.7 %all_to_all.14 = bf16[4,4,4096]{2,1,0:T(4,128)(2,1)} all-to-all(bf16[4,4,4096]{2,1,0:T(4,128)(2,1)S(1)} %bitcast.44), channel_id=1, replica_groups=mesh['expert'=4,'feat'=32] {'expert'}, dimensions={0} | all-to-all | bytes 262144 | tf_op jit(solution)/shard_map/all_to_all | solution.py:92
  19.0 0.0 all-gather.3.cloned.1.call-update
  19.0 0.0 reduce-scatter.2.cloned.1.call-start
  19.1 0.7 exp.10
  19.8 48.0 %all-gather.3.cloned.1.call-done = bf16[128,4,4096]{2,1,0:T(4,128)(2,1)} async-done(((bf16[4,4,4096]{2,1,0:T(4,128)(2,1)}), bf16[128,4,4096]{2,1,0:T(4,128)(2,1)}) %all-gather.3.cloned.1.call-update) | async-done | bytes 4194320 | tf_op jit(solution)/shard_map/all_gather | solution.py:96
  67.8 6.9 %reshape.68 = bf16[512,4096]{1,0:T(8,128)(2,1)} reshape(bf16[128,4,4096]{2,1,0:T(4,128)(2,1)} %all-gather.3.cloned.1.call-done) | data formatting | bytes 8388608 | tf_op jit(solution)/shard_map/reshape | solution.py:100
  74.6 4.9 %fusion.2 = f32[512,256]{1,0:T(8,128)S(1)} fusion(bf16[512,4096]{1,0:T(8,128)(2,1)} %reshape.68, f32[4096,256]{1,0:T(8,128)} %param.16), kind=kOutput, calls=%fused_computation.10 | convolution fusion | flops 1076887552 | bytes 8912896 | tf_op jit(solution)/shard_map/dot_general | solution.py:71
  79.5 0.0 copy-done.2
  79.5 1.0 copy-done.7
  80.6 0.0 copy-done.8
  80.6 1.3 fusion.6
  81.8 0.9 copy-done.5
  82.8 4.6 %fusion.11 = f32[512,4096]{1,0:T(8,128)} fusion(f32[256,4096]{1,0:T(8,128)S(1)} %copy-done.5, f32[512,256]{1,0:T(8,128)S(1)} %fusion.6, f32[256]{0:T(256)S(1)} %exp.10), kind=kOutput, calls=%fused_computation.23 | convolution fusion | flops 1077936128 | bytes 13108224 | tf_op jit(solution)/shard_map/dot_general | solution.py:71
  87.3 4.5 %fusion.41 = f32[512,4096]{1,0:T(8,128)} fusion(f32[256,4096]{1,0:T(8,128)S(1)} %copy-done.5, f32[512,256]{1,0:T(8,128)S(1)} %fusion.6, f32[256]{0:T(256)S(1)} %exp.10), kind=kOutput, calls=%fused_computation.72 | convolution fusion | flops 1076887552 | bytes 13108224 | tf_op jit(solution)/shard_map/dot_general | solution.py:71
  91.9 0.0 copy-done.12
  91.9 1.4 fusion.49
  93.3 0.0 copy-done
  93.3 8.7 %fusion.8 = f32[512,4096]{1,0:T(8,128)} fusion(bf16[224,4096]{1,0:T(8,128)(2,1)S(1)} %copy-done, bf16[512,4096]{1,0:T(8,128)(2,1)} %reshape.68, bf16[4096,224]{0,1:T(8,128)(2,1)} %param.14, f32[512,224]{0,1:T(8,128)S(1)} %fusion.49), kind=kOutput, calls=%fused_computation.17 | convolution fusion | flops 1879736320 | bytes 16711680 | tf_op jit(solution)/shard_map/dot_general | solution.py:105
  102.0 14.3 %add_subtract_fusion = f32[512,4096]{1,0:T(8,128)} fusion(f32[512,4096]{1,0:T(8,128)} %fusion.8, f32[512,4096]{1,0:T(8,128)} %fusion.41, f32[512,4096]{1,0:T(8,128)} %fusion.11, f32[256,4096]{1,0:T(8,128)} %param.19, f32[512,256]{1,0:T(8,128)S(1)} %fusion.6, f32[256]{0:T(256)S(1)} %exp.10), kind=kOutput, calls=%fused_computation | convolution fusion | flops 1083310080 | bytes 38274048 | tf_op jit(solution)/shard_map/dot_general | solution.py:71
  116.3 0.0 reduce-scatter.2.cloned.1.call-update
  116.3 0.7 copy-done.10
  117.0 0.0 copy-done.11
  117.0 0.1 fusion.33
  117.1 0.6 copy.45
  117.7 4.0 %all-to-all-start.1 = ((bf16[4,1,4]{2,1,0:T(2,128)(2,1)}), bf16[4,1,4]{2,1,0:T(2,128)(2,1)S(1)}, u32[]{:S(2)}, u32[]{:S(2)}) async-start(bf16[4,1,4]{2,1,0:T(2,128)(2,1)} %copy.45), calls=%async_computation.1 | async-start | bytes 4096 | tf_op jit(solution)/shard_map/all_to_all | solution.py:93
  121.7 0.0 all-gather.5.cloned.1.call-start
  121.7 4.0 %all-to-all-done.1 = bf16[4,1,4]{2,1,0:T(2,128)(2,1)S(1)} async-done(((bf16[4,1,4]{2,1,0:T(2,128)(2,1)}), bf16[4,1,4]{2,1,0:T(2,128)(2,1)S(1)}, u32[]{:S(2)}, u32[]{:S(2)}) %all-to-all-start.1) | async-done | bytes 64 | tf_op jit(solution)/shard_map/all_to_all | solution.py:93
  125.7 1.7 collective-permute-start
  127.4 0.8 collective-permute-done
  128.3 1.0 collective-permute-start.1
  129.2 1.6 collective-permute-done.1
  130.8 2.1 collective-permute-start.2
  132.9 2.2 collective-permute-done.2
  135.1 0.1 copy.52
  135.2 0.7 collective-permute-start.3
  135.9 0.1 copy.51
  136.0 1.7 collective-permute-done.3
  137.7 0.1 reshape.72
  137.8 1.7 collective-permute-start.4
  139.5 0.1 stack_reshape.15
  139.6 2.2 collective-permute-done.4
  141.8 64.7 %reduce-scatter.2.cloned.1.call-done = f32[16,4096]{1,0:T(8,128)} async-done(((f32[512,4096]{1,0:T(8,128)}), f32[16,4096]{1,0:T(8,128)}) %reduce-scatter.2.cloned.1.call-update) | async-done | bytes 262160 | tf_op jit(solution)/shard_map/reduce_scatter | solution.py:118
  206.5 1.2 collective-permute-start.5
  207.7 0.1 copy.50
  207.8 0.1 reshape.73
  207.9 0.1 dynamic-slice_multiply_fusion
  208.0 3.9 %collective-permute-done.5 = f32[16,4096]{1,0:T(8,128)S(1)} collective-permute-done((f32[16,4096]{1,0:T(8,128)}, f32[16,4096]{1,0:T(8,128)S(1)}, u32[]{:S(2)}, u32[]{:S(2)}) %collective-permute-start.5) | collective-permute-done | bytes 262176 | tf_op jit(solution)/shard_map/ppermute | solution.py:40
  211.9 1.7 multiply_convert_fusion
  213.6 0.0 all-gather.5.cloned.1.call-update
  213.6 49.1 %all-gather.5.cloned.1.call-done = bf16[512,4096]{1,0:T(8,128)(2,1)} async-done(((bf16[16,4096]{1,0:T(8,128)(2,1)}), bf16[512,4096]{1,0:T(8,128)(2,1)}) %all-gather.5.cloned.1.call-update) | async-done | bytes 4194320 | tf_op jit(solution)/shard_map/all_gather | solution.py:123
  262.8 4.9 %fusion.9 = f32[512,256]{1,0:T(8,128)S(1)} fusion(bf16[512,4096]{1,0:T(8,128)(2,1)} %all-gather.5.cloned.1.call-done, f32[256,4096]{1,0:T(8,128)} %param.19), kind=kOutput, calls=%fused_computation.22 | convolution fusion | flops 1076887552 | bytes 8912896 | tf_op jit(solution)/shard_map/dot_general | solution.py:71
  267.7 0.0 copy-done.4
  267.7 1.0 copy-done.6
  268.7 2.0 fusion.47
  270.7 0.6 negate_multiply_fusion
  271.3 1.3 fusion.23
  272.6 3.3 %convolution_add_fusion.1 = f32[4096,256]{1,0:T(8,128)} fusion(f32[4096,256]{1,0:T(8,128)S(1)} %fusion.23, bf16[512,4096]{1,0:T(8,128)(2,1)S(1)} %copy-done.3, f32[512,256]{1,0:T(8,128)S(1)} %get-tuple-element.5), kind=kOutput, calls=%fused_computation.6 | convolution fusion | flops 1075183616 | bytes 13107200 | tf_op jit(solution)/shard_map/dot_general | solution.py:71
  275.9 1.4 fusion.25
  277.3 3.5 %convolution_add_fusion = f32[256,4096]{1,0:T(8,128)} fusion(f32[256,4096]{1,0:T(8,128)S(1)} %fusion.25, bf16[512,4096]{1,0:T(8,128)(2,1)S(1)} %copy-done.4, f32[512,256]{1,0:T(8,128)S(1)} %fusion.6, f32[256]{0:T(256)S(1)} %exp.10), kind=kOutput, calls=%fused_computation.5 | convolution fusion | flops 1075838976 | bytes 13108224 | tf_op jit(solution)/shard_map/dot_general | solution.py:71
  (33 shorter events, 0.2 us)
Async XLA Ops:
  7.2 86.1 %copy-start = (bf16[224,4096]{1,0:T(8,128)(2,1)S(1)}, bf16[224,4096]{1,0:T(8,128)(2,1)}, u32[]{:S(2)}) copy-start(bf16[224,4096]{1,0:T(8,128)(2,1)} %param.15) | copy-start | bytes 5505028
  7.2 60.6 %all-gather.3.cloned.1.call-start = ((), (), s32[]{:S(2)}) async-start(), calls=%async_computation.3 | async-start | bytes 4325376 | tf_op jit(solution)/shard_map/all_gather | solution.py:96
  19.0 187.5 %reduce-scatter.2.cloned.1.call-start = ((), (), s32[]{:S(2)}) async-start(), calls=%async_computation.4 | async-start | bytes 8650752 | tf_op jit(solution)/shard_map/reduce_scatter | solution.py:118
  74.6 4.9 %copy-start.2 = (bf16[512,4096]{1,0:T(8,128)(2,1)S(1)}, bf16[512,4096]{1,0:T(8,128)(2,1)}, u32[]{:S(2)}) copy-start(bf16[512,4096]{1,0:T(8,128)(2,1)} %reshape.68) | copy-start | bytes 12582916
  74.6 5.9 %copy-start.7 = (f32[4096,256]{1,0:T(8,128)S(1)}, f32[4096,256]{1,0:T(8,128)}, u32[]{:S(2)}) copy-start(f32[4096,256]{1,0:T(8,128)} %param.16) | copy-start | bytes 12582916
  74.6 5.9 %copy-start.8 = (f32[256]{0:T(256)S(1)}, f32[256]{0:T(256)}, u32[]{:S(2)}) copy-start(f32[256]{0:T(256)} %param.17) | copy-start | bytes 3076
  80.6 2.2 copy-start.5
  87.3 4.5 %copy-start.12 = (bf16[4096,224]{0,1:T(8,128)(2,1)S(1)}, bf16[4096,224]{0,1:T(8,128)(2,1)}, u32[]{:S(2)}) copy-start(bf16[4096,224]{0,1:T(8,128)(2,1)} %param.13) | copy-start | bytes 5505028
  116.3 0.7 copy-start.10
  116.3 0.7 copy-start.11
  117.7 8.0 %all-to-all-start.1 = ((bf16[4,1,4]{2,1,0:T(2,128)(2,1)}), bf16[4,1,4]{2,1,0:T(2,128)(2,1)S(1)}, u32[]{:S(2)}, u32[]{:S(2)}) async-start(bf16[4,1,4]{2,1,0:T(2,128)(2,1)} %copy.45), calls=%async_computation.1 | async-start | bytes 4096 | tf_op jit(solution)/shard_map/all_to_all | solution.py:93
  121.7 141.1 %all-gather.5.cloned.1.call-start = ((), (), s32[]{:S(2)}) async-start(), calls=%async_computation.5 | async-start | bytes 4325376 | tf_op jit(solution)/shard_map/all_gather | solution.py:123
  125.7 2.5 collective-permute-start
  128.3 2.5 collective-permute-start.1
  130.8 4.2 %collective-permute-start.2 = (bf16[4,4,4]{2,1,0:T(4,128)(2,1)S(1)}, bf16[4,4,4]{2,1,0:T(4,128)(2,1)S(1)}, u32[]{:S(2)}, u32[]{:S(2)}) collective-permute-start(bf16[4,4,4]{2,1,0:T(4,128)(2,1)S(1)} %bitcast.47), channel_id=1, source_target_pairs={{0,4},{1,5},{2,6},{3,7},{4,0},{5,1},{6,2},{7,3},{8,12},{9,13},{10,... | collective-permute-start | bytes 392 | tf_op jit(solution)/shard_map/ppermute | solution.py:22
  135.2 2.5 collective-permute-start.3
  137.8 4.0 %collective-permute-start.4 = (bf16[16,4,4]{0,2,1:T(4,128)(2,1)S(1)}, bf16[16,4,4]{0,2,1:T(4,128)(2,1)S(1)}, u32[]{:S(2)}, u32[]{:S(2)}) collective-permute-start(bf16[16,4,4]{0,2,1:T(4,128)(2,1)S(1)} %reshape.72), channel_id=1, source_target_pairs={{0,16},{1,17},{2,18},{3,19},{4,20},{5,21},{6,22},{7,23},{8,24},{9,... | collective-permute-start | bytes 1544 | tf_op jit(solution)/shard_map/ppermute | solution.py:22
  206.5 5.4 %collective-permute-start.5 = (f32[16,4096]{1,0:T(8,128)}, f32[16,4096]{1,0:T(8,128)S(1)}, u32[]{:S(2)}, u32[]{:S(2)}) collective-permute-start(f32[16,4096]{1,0:T(8,128)} %reduce-scatter.2.cloned.1.call-done), channel_id=1, source_target_pairs={{0,32},{32,0},{64,96},{96,64},{1,33},{33,1},{65,97},{97,65},{2,34}... | collective-permute-start | bytes 786440 | tf_op jit(solution)/shard_map/ppermute | solution.py:40
  262.8 4.9 %copy-start.4 = (bf16[512,4096]{1,0:T(8,128)(2,1)S(1)}, bf16[512,4096]{1,0:T(8,128)(2,1)}, u32[]{:S(2)}) copy-start(bf16[512,4096]{1,0:T(8,128)(2,1)} %all-gather.5.cloned.1.call-done) | copy-start | bytes 12582916
  262.8 5.9 %copy-start.6 = (f32[256,4096]{1,0:T(8,128)S(1)}, f32[256,4096]{1,0:T(8,128)}, u32[]{:S(2)}) copy-start(f32[256,4096]{1,0:T(8,128)} %param.19) | copy-start | bytes 12582916
  268.7 2.0 copy-start.9
  268.7 2.6 copy-start.3
  275.9 4.9 %copy-start.1 = (bf16[224,4096]{1,0:T(8,128)(2,1)S(1)}, bf16[224,4096]{1,0:T(8,128)(2,1)}, u32[]{:S(2)}) copy-start(bf16[224,4096]{1,0:T(8,128)(2,1)} %param.15) | copy-start | bytes 5505028
Sparse Core Ops, SparseCore 0:
  19.1 48.5 all-gather.2
  116.5 89.9 reduce-scatter.1
  213.7 48.9 all-gather.4
